TPU v7x, 32 devices: a whole 2x2x4 slice. The times are simulated.
32 devices in a mesh: dp: 4 (over z), expert: 8 (over y, x, core).
Axes of the slice: x: 2, y: 2, z: 4, core: 2. Of those that a mesh axis runs over, the one named last changes fastest.
Arguments:
- tokens: bfloat16 [4096, 2048], P(('dp', 'expert')), may hold values from -6 to 6
- grad_mixed: bfloat16 [4096, 2048], P(('dp', 'expert')), may hold values from -0.059814453 to 0.059814453
- expert_ids: int32 [4096, 8], P(('dp', 'expert')), may hold values from 0 to 15, all different within a row; in each aligned block of 128 rows (0 to 127, 128 to 255, ...) at most 128 rows name the same one
- gate_probs: bfloat16 [4096, 8], P(('dp', 'expert')), may hold values from 0.019897461 to 0.25
- gate_proj: bfloat16 [16, 2048, 768], P('expert'), may hold values from -0.125 to 0.125
- up_proj: bfloat16 [16, 2048, 768], P('expert'), may hold values from -0.125 to 0.125
- down_proj: bfloat16 [16, 768, 2048], P('expert'), may hold values from -0.21875 to 0.21875
- share_down: float32 [4, 4, 4], replicated, may hold values from -3 to 3
- share_up: float32 [4, 4, 4], replicated, may hold values from -3 to 3
- factor_down: float32 [16, 4, 512, 16], P('expert'), may hold values from -0.125 to 0.125
- factor_up: float32 [16, 4, 16, 192], P('expert'), may hold values from -0.5 to 0.5
Outputs:
- mixed: bfloat16 [4096, 2048], P(('dp', 'expert'))
- grad_factor_down: float32 [16, 4, 512, 16], P('expert')
- grad_factor_up: float32 [16, 4, 16, 192], P('expert')
- grad_share_down: float32 [4, 4, 4], replicated
- grad_share_up: float32 [4, 4, 4], replicated
Inputs may be any that keep to these rules, and one draw needn't show every extreme that they name: `expert_ids`: each row names 8 different experts. In the rows of one device (aligned blocks of 128 rows) no expert is named more than 128 times, a bound that some block reaches.
All inputs are finite; a program needn't handle non-finite values.
Results may differ from a plain program's by a relative error of at most 0.0096.
Values may be sent and summed in bfloat16 or wider, within the bound.
A program may use at most 192 MiB of HBM per device.

v0:
```python
from functools import partial

import jax
import jax.numpy as jnp
from jax import lax
from jax.sharding import PartitionSpec as P


def routed_slots(ids_block, first_expert, expert_span, capacity):
    flat_ids = ids_block.reshape(-1).astype(jnp.int32)
    slot_count = flat_ids.shape[0]
    local_ids = flat_ids - first_expert
    onehot = local_ids[:, None] == jnp.arange(expert_span, dtype=jnp.int32)[None, :]
    order = jnp.arange(slot_count, dtype=jnp.int32)
    earlier = (order[:, None] > order[None, :]).astype(jnp.bfloat16)
    before = jnp.dot(earlier, onehot.astype(jnp.bfloat16), preferred_element_type=jnp.float32)
    rank_in = jnp.sum(jnp.where(onehot, before, 0.0), axis=1).astype(jnp.int32)
    inside = (local_ids >= 0) & (local_ids < expert_span)
    position = jnp.where(inside, local_ids * capacity + rank_in, -1)
    targets = jnp.arange(expert_span * capacity, dtype=jnp.int32)
    match = position[:, None] == targets[None, :]
    found = jnp.max(jnp.where(match, order[:, None], -1), axis=0)
    slot_map = jnp.where(found < 0, slot_count, found)
    return (slot_map, position)


def expand(factor_a, factor_b):
    kron_n, rows_b, cols_b = factor_b.shape
    blocks = jnp.einsum("iac,ibd->abcd", factor_a, factor_b, precision=lax.Precision.HIGHEST)
    return blocks.reshape(kron_n * rows_b, kron_n * cols_b)


def factor_grads(factor_a, factor_b, grad_w):
    kron_n, rows_b, cols_b = factor_b.shape
    blocks = grad_w.reshape(kron_n, rows_b, kron_n, cols_b)
    grad_b = jnp.einsum("iac,abcd->ibd", factor_a, blocks, precision=lax.Precision.HIGHEST)
    grad_a = jnp.einsum("ibd,abcd->iac", factor_b, blocks, precision=lax.Precision.HIGHEST)
    return (grad_b, grad_a)


def expert_forward(row_data, gate_mat, up_mat, down_mat, adapter_down, adapter_up):
    lowrank = jnp.dot(row_data, adapter_down, preferred_element_type=jnp.float32).astype(
        jnp.bfloat16
    )
    gate_pre = jnp.dot(row_data, gate_mat, preferred_element_type=jnp.float32) + jnp.dot(
        lowrank, adapter_up, preferred_element_type=jnp.float32
    )
    up_pre = jnp.dot(row_data, up_mat, preferred_element_type=jnp.float32)
    hidden = (jax.nn.silu(gate_pre) * up_pre).astype(jnp.bfloat16)
    result = jnp.dot(hidden, down_mat, preferred_element_type=jnp.float32).astype(jnp.bfloat16)
    return (result, lowrank, gate_pre, up_pre)


def expert_backward(row_data, weighted, down_mat, adapter_up, lowrank, gate_pre, up_pre):
    grad_hidden = lax.dot_general(
        weighted, down_mat, (((1,), (1,)), ((), ())), preferred_element_type=jnp.float32
    )
    sigmoid_g = jax.nn.sigmoid(gate_pre)
    grad_gate = (grad_hidden * up_pre * sigmoid_g * (1.0 + gate_pre * (1.0 - sigmoid_g))).astype(
        jnp.bfloat16
    )
    grad_aup = lax.dot_general(
        lowrank, grad_gate, (((0,), (0,)), ((), ())), preferred_element_type=jnp.float32
    )
    grad_low = lax.dot_general(
        grad_gate, adapter_up, (((1,), (1,)), ((), ())), preferred_element_type=jnp.float32
    ).astype(jnp.bfloat16)
    grad_adown = lax.dot_general(
        row_data, grad_low, (((0,), (0,)), ((), ())), preferred_element_type=jnp.float32
    )
    return (grad_adown, grad_aup)


def on_device(
    tokens,
    grad_mixed,
    expert_ids,
    gate_probs,
    gate_proj,
    up_proj,
    down_proj,
    share_down,
    share_up,
    factor_down,
    factor_up,
):
    tok_rows, top_k = expert_ids.shape
    slot_count = tok_rows * top_k
    local_experts = gate_proj.shape[0]
    groups = lax.axis_size("expert")
    expert_count = local_experts * groups
    capacity = 2 * slot_count // expert_count
    model_width = tokens.shape[1]
    zero_row = jnp.zeros((1, model_width), tokens.dtype)
    own_map, own_position = routed_slots(expert_ids, 0, expert_count, capacity)
    all_tokens, all_ids = (
        lax.all_gather(tokens, "expert", axis=0, tiled=True),
        lax.all_gather(expert_ids, "expert", axis=0, tiled=True),
    )
    first_local = lax.axis_index("expert") * local_experts
    tables, unused = jax.vmap(
        partial(
            routed_slots, first_expert=first_local, expert_span=local_experts, capacity=capacity
        )
    )(all_ids.reshape(groups, tok_rows, top_k))
    own_slots = tables.reshape(groups, local_experts, capacity).transpose(1, 0, 2)
    source = jnp.arange(groups, dtype=jnp.int32)[None, :, None] * slot_count
    global_slot = jnp.where(own_slots < slot_count, own_slots + source, groups * slot_count)
    padded = jnp.concatenate([all_tokens, zero_row], axis=0)
    received = padded[(global_slot // top_k).reshape(-1)].reshape(
        local_experts, groups * capacity, model_width
    )
    outputs = []
    stashed = []
    for member in range(local_experts):
        adapter_down = expand(share_down, factor_down[member]).astype(jnp.bfloat16)
        adapter_up = expand(share_up, factor_up[member]).astype(jnp.bfloat16)
        result, lowrank, gate_pre, up_pre = expert_forward(
            received[member],
            gate_proj[member],
            up_proj[member],
            down_proj[member],
            adapter_down,
            adapter_up,
        )
        outputs.append(result)
        stashed.append((lowrank, gate_pre, up_pre, adapter_up))
    returned = lax.all_to_all(jnp.stack(outputs), "expert", split_axis=1, concat_axis=0, tiled=True)
    picked = returned.reshape(expert_count * capacity, model_width)[own_position].astype(
        jnp.float32
    )
    mixed = jnp.sum(
        picked.reshape(tok_rows, top_k, model_width) * gate_probs.astype(jnp.float32)[:, :, None],
        axis=1,
    ).astype(jnp.bfloat16)
    gate_pad = jnp.concatenate([gate_probs.reshape(-1), jnp.zeros((1,), gate_probs.dtype)])
    grad_pad = jnp.concatenate([grad_mixed, zero_row], axis=0)
    weighted = (
        gate_pad[own_map].astype(jnp.float32)[:, None]
        * grad_pad[own_map // top_k].astype(jnp.float32)
    ).astype(jnp.bfloat16)
    grad_slots = lax.all_to_all(
        weighted.reshape(expert_count, capacity, model_width),
        "expert",
        split_axis=0,
        concat_axis=1,
        tiled=True,
    )
    bdown_list = []
    bup_list = []
    adown_total = jnp.zeros(share_down.shape, jnp.float32)
    aup_total = jnp.zeros(share_up.shape, jnp.float32)
    for member in range(local_experts):
        lowrank, gate_pre, up_pre, adapter_up = stashed[member]
        grad_adown, grad_aup = expert_backward(
            received[member],
            grad_slots[member],
            down_proj[member],
            adapter_up,
            lowrank,
            gate_pre,
            up_pre,
        )
        bdown_grad, adown_grad = factor_grads(share_down, factor_down[member], grad_adown)
        bup_grad, aup_grad = factor_grads(share_up, factor_up[member], grad_aup)
        bdown_list.append(bdown_grad)
        bup_list.append(bup_grad)
        adown_total = adown_total + adown_grad
        aup_total = aup_total + aup_grad
    bdown_all = jnp.stack(bdown_list)
    bup_all = jnp.stack(bup_list)
    bdown_all, bup_all, adown_total, aup_total = lax.psum(
        (bdown_all, bup_all, adown_total, aup_total), "dp"
    )
    adown_total, aup_total = lax.psum((adown_total, aup_total), "expert")
    return (mixed, bdown_all, bup_all, adown_total, aup_total)


def solution(mesh):
    return jax.shard_map(
        on_device,
        mesh=mesh,
        in_specs=(
            P(("dp", "expert"), None),
            P(("dp", "expert"), None),
            P(("dp", "expert"), None),
            P(("dp", "expert"), None),
            P("expert", None, None),
            P("expert", None, None),
            P("expert", None, None),
            P(),
            P(),
            P("expert", None, None, None),
            P("expert", None, None, None),
        ),
        out_specs=(
            P(("dp", "expert"), None),
            P("expert", None, None, None),
            P("expert", None, None, None),
            P(),
            P(),
        ),
        check_vma=False,
    )
```

profile of v0, /device:TPU:0, one launch (start us, length us, event | category | flops | bytes accessed | tf_op | source)
XLA Modules:
  0.0 396.4 jit_solution(1122672865154783096)
XLA Ops:
  12.8 11.0 %gather_fusion.3 = bf16[2048,2048]{1,0:T(8,128)(2,1)} fusion(bf16[129,2048]{1,0:T(8,128)(2,1)S(1)} %concatenate.11, s32[2048]{0:T(1024)S(1)} %broadcast_clamp_fusion), kind=kCustom, calls=%fused_computation.3 | custom fusion | bytes 16785408 | tf_op jit(solution)/shard_map/gather | solution.py:140
  23.8 13.1 %gather_fusion.2 = bf16[2048]{0:T(1024)(128)(2,1)S(1)} fusion(bf16[1025]{0:T(1024)(128)(2,1)S(1)} %pad_maximum_fusion.3, s32[2048]{0:T(1024)S(1)} %broadcast_clamp_fusion.1), kind=kCustom, calls=%fused_computation.2 | custom fusion | bytes 16384 | tf_op jit(solution)/shard_map/gather | solution.py:139
  36.9 8.1 %fusion = bf16[16,128,2048]{2,1,0:T(8,128)(2,1)} fusion(bf16[16,128,2048]{2,1,0:T(8,128)(2,1)} %bitcast.234, f32[16,128]{1,0:T(8,128)S(1)} %bitcast_convert_fusion), kind=kLoop, calls=%fused_computation.5 | loop fusion | flops 12582912 | bytes 16785408 | tf_op jit(solution)/shard_map/convert_element_type | solution.py:141
  45.0 5.4 %all-to-all-start.1 = ((bf16[16,128,2048]{2,1,0:T(8,128)(2,1)}), bf16[16,128,2048]{2,1,0:T(8,128)(2,1)}, u32[]{:S(2)}, u32[]{:S(2)}) async-start(bf16[16,128,2048]{2,1,0:T(8,128)(2,1)} %fusion), calls=%async_computation.1 | async-start | bytes 16777216 | tf_op jit(solution)/shard_map/all_to_all | solution.py:142
  51.1 96.9 %all_gather.7 = s32[1024,8]{0,1:T(8,128)S(1)} all-gather(s32[128,8]{0,1:T(8,128)S(1)} %copy-done.19), channel_id=1, replica_groups=mesh['dp'=4,'expert'=8] {'expert'}, dimensions={0}, use_global_device_ids=true | all-gather | bytes 36864 | tf_op jit(solution)/shard_map/all_gather | solution.py:98
  156.7 4.7 %concatenate.9 = bf16[1025,2048]{1,0:T(8,128)(2,1)} pad(bf16[1024,2048]{1,0:T(8,128)(2,1)} %all-gather.2.cloned.1.call-done, bf16[]{:T(256)} %constant.19.clone.1), padding=0_1x0_0 | pad | bytes 8392706 | tf_op jit(solution)/shard_map/concatenate | solution.py:109
  161.4 19.5 %gather_fusion = bf16[2048,2048]{1,0:T(8,128)(2,1)} fusion(bf16[1025,2048]{1,0:T(8,128)(2,1)} %concatenate.9, s32[2048]{0:T(1024)S(1)} %broadcast_clamp_fusion.2), kind=kCustom, calls=%fused_computation | custom fusion | bytes 16785408 | tf_op jit(solution)/shard_map/gather | solution.py:110
  180.9 3.7 fusion.51
  187.0 5.4 %fusion.11 = f32[1024,768]{1,0:T(8,128)S(1)} fusion(bf16[2,2048,768]{2,1,0:T(8,128)(2,1)} %param.15, bf16[2048,2048]{1,0:T(8,128)(2,1)S(1)} %copy-done), kind=kOutput, calls=%fused_computation.24 | convolution fusion | flops 3221225472 | bytes 10485760 | tf_op jit(solution)/shard_map/dot_general | solution.py:45
  197.2 5.1 %fusion.9 = f32[1024,768]{1,0:T(8,128)} fusion(bf16[2,2048,768]{2,1,0:T(8,128)(2,1)S(1)} %bitcast.254, bf16[2048,2048]{1,0:T(8,128)(2,1)S(1)} %copy-done), kind=kOutput, calls=%fused_computation.22 | convolution fusion | flops 3221225472 | bytes 10485760 | tf_op jit(solution)/shard_map/dot_general | solution.py:48
  209.7 5.1 %convert_bitcast_fusion = bf16[1,1024,2048]{2,1,0:T(8,128)(2,1)} fusion(bf16[2,768,2048]{2,1,0:T(8,128)(2,1)S(1)} %bitcast.256, f32[1024,768]{1,0:T(8,128)S(1)} %copy-done.24, f32[1024,768]{1,0:T(8,128)S(1)} %convolution_add_fusion), kind=kOutput, calls=%fused_computation.13 | convolution fusion | flops 3228041216 | bytes 13631488 | tf_op jit(solution)/shard_map/dot_general | solution.py:50
  214.7 6.2 %pad_maximum_fusion = bf16[2,1024,2048]{2,1,0:T(8,128)(2,1)} fusion(bf16[1,1024,2048]{2,1,0:T(8,128)(2,1)} %convert_bitcast_fusion, bf16[1,1024,2048]{2,1,0:T(8,128)(2,1)S(1)} %convert_bitcast_fusion.1), kind=kLoop, calls=%fused_computation.6 | loop fusion | flops 4194304 | bytes 16777216 | tf_op jit(solution)/shard_map/stack | solution.py:128
  220.9 16.4 %copy.114 = bf16[2,1024,2048]{2,0,1:T(2,128)(2,1)} copy(bf16[2,1024,2048]{2,1,0:T(8,128)(2,1)} %pad_maximum_fusion) | data formatting | bytes 16777216 | tf_op jit(solution)/shard_map/stack | solution.py:128
  237.3 5.0 %all-to-all-start = ((bf16[2,1024,2048]{2,0,1:T(2,128)(2,1)}), bf16[2,1024,2048]{2,0,1:T(2,128)(2,1)}, u32[]{:S(2)}, u32[]{:S(2)}) async-start(bf16[2,1024,2048]{2,0,1:T(2,128)(2,1)} %copy.114), calls=%async_computation | async-start | bytes 16777216 | tf_op jit(solution)/shard_map/all_to_all | solution.py:128
  243.3 5.5 %fusion.100 = (bf16[1,8,128,2048]{3,2,0,1:T(8,128)(2,1)}, bf16[1,8,128,2048]{3,2,0,1:T(8,128)(2,1)S(1)}) fusion(bf16[2,8,128,2048]{3,2,0,1:T(8,128)(2,1)} %bitcast.46), kind=kLoop, calls=%fused_computation.154 | loop fusion | bytes 16777216 | tf_op jit(solution)/shard_map/slice | solution.py:157
  250.1 6.1 %multiply_convert_fusion = bf16[1024,768]{1,0:T(8,128)(2,1)S(1)} fusion(f32[1024,768]{1,0:T(8,128)S(1)} %copy-done.3, f32[1024,768]{1,0:T(8,128)S(1)} %copy-done.25, bf16[1024,2048]{1,0:T(8,128)(2,1)S(1)} %bitcast.236, bf16[2,768,2048]{2,1,0:T(8,128)(2,1)} %param.17), kind=kOutput, calls=%fused_computation.33 | convolution fusion | flops 3229089792 | bytes 15204352 | tf_op jit(solution)/shard_map/dot_general | solution.py:55
  256.8 9.0 %multiply_convert_fusion.1 = bf16[1024,768]{1,0:T(8,128)(2,1)S(1)} fusion(f32[1024,768]{1,0:T(8,128)} %copy-done.1, f32[1024,768]{1,0:T(8,128)} %copy-done.23, bf16[1024,2048]{1,0:T(8,128)(2,1)} %bitcast.235, bf16[2,768,2048]{2,1,0:T(8,128)(2,1)} %param.17), kind=kOutput, calls=%fused_computation.34 | convolution fusion | flops 3229089792 | bytes 15204352 | tf_op jit(solution)/shard_map/dot_general | solution.py:55
  268.7 4.4 %fusion.28 = f32[2048,64]{0,1:T(8,128)} fusion(bf16[2048,2048]{1,0:T(8,128)(2,1)} %gather_fusion, bf16[1024,768]{1,0:T(8,128)(2,1)S(1)} %multiply_convert_fusion, bf16[64,768]{1,0:T(8,128)(2,1)} %copy-done.7), kind=kOutput, calls=%fused_computation.47 | convolution fusion | flops 369164288 | bytes 6389760 | tf_op jit(solution)/shard_map/dot_general | solution.py:68
  274.6 4.4 %fusion.34 = f32[2048,64]{0,1:T(8,128)} fusion(bf16[2048,2048]{1,0:T(8,128)(2,1)} %gather_fusion, bf16[1024,768]{1,0:T(8,128)(2,1)S(1)} %multiply_convert_fusion.1, bf16[64,768]{1,0:T(8,128)(2,1)} %copy-done.8), kind=kOutput, calls=%fused_computation.53 | convolution fusion | flops 369164288 | bytes 6389760 | tf_op jit(solution)/shard_map/dot_general | solution.py:68
  289.4 19.9 %all-reduce.3 = (f32[4,4,4]{0,1,2:T(4,128)S(1)}, f32[4,4,4]{0,2,1:T(4,128)S(1)}) all-reduce(f32[4,4,4]{0,1,2:T(4,128)S(1)} %fusion.68, f32[4,4,4]{0,2,1:T(4,128)S(1)} %fusion.70), channel_id=1, replica_groups=mesh['dp'=4,'expert'=8] {'dp'}, use_global_device_ids=true, to_apply=%region_7.8 | all-reduce | flops 128 | bytes 1024 | tf_op jit(solution)/shard_map/psum | solution.py:172
  309.3 43.9 %all-reduce.2 = (f32[4,4,4]{0,1,2:T(4,128)S(1)}, f32[4,4,4]{0,2,1:T(4,128)S(1)}) all-reduce(f32[4,4,4]{0,1,2:T(4,128)S(1)} %get-tuple-element.27, f32[4,4,4]{0,2,1:T(4,128)S(1)} %get-tuple-element.28), channel_id=1, replica_groups=mesh['dp'=4,'expert'=8] {'expert'}, use_global_device_ids=true, to_apply=%region_8.9 | all-reduce | flops 128 | bytes 1024 | tf_op jit(solution)/shard_map/psum | solution.py:175
  357.9 10.6 %copy.115 = bf16[2,8,128,2048]{3,2,0,1:T(8,128)(2,1)} copy(bf16[2,8,128,2048]{3,0,2,1:T(2,128)(2,1)} %bitcast.34) | data formatting | bytes 16777216 | tf_op jit(solution)/shard_map/all_to_all | solution.py:128
  368.5 13.3 %gather_fusion.1 = bf16[1024,2048]{1,0:T(8,128)(2,1)} fusion(bf16[2048,2048]{1,0:T(8,128)(2,1)} %bitcast.233, s32[1024]{0:T(1024)S(1)} %copy-done.21), kind=kCustom, calls=%fused_computation.1 | custom fusion | bytes 8392704 | tf_op jit(solution)/shard_map/gather | solution.py:129
  381.8 7.3 %fusion.1 = bf16[128,2048]{1,0:T(8,128)(2,1)} fusion(bf16[1024,2048]{1,0:T(8,128)(2,1)} %gather_fusion.1, f32[128,8]{1,0:T(8,128)S(1)} %copy-done.15), kind=kLoop, calls=%fused_computation.8 | loop fusion | flops 6029312 | bytes 4722688 | tf_op jit(solution)/shard_map/reduce_sum | solution.py:132
  (151 shorter events, 51.2 us)
Async XLA Ops:
  7.2 149.5 %all-gather.2.cloned.1.call-start = ((), (), s32[]{:S(2)}) async-start(), calls=%async_computation.2 | async-start | bytes 4718592 | tf_op jit(solution)/shard_map/all_gather | solution.py:97
  45.0 6.2 %copy-start.19 = (s32[128,8]{0,1:T(8,128)S(1)}, s32[128,8]{0,1:T(8,128)}, u32[]{:S(2)}) copy-start(s32[128,8]{0,1:T(8,128)} %param.13) | copy-start | bytes 12292
  45.0 103.5 %copy-start.20 = (f32[4,4,4]{2,1,0:T(4,128)S(1)}, f32[4,4,4]{2,1,0:T(4,128)}, u32[]{:S(2)}) copy-start(f32[4,4,4]{2,1,0:T(4,128)} %param.18) | copy-start | bytes 772
  45.0 103.7 %copy-start.16 = (f32[2,4,512,16]{2,3,1,0:T(8,128)S(1)}, f32[2,4,512,16]{2,3,1,0:T(8,128)}, u32[]{:S(2)}) copy-start(f32[2,4,512,16]{2,3,1,0:T(8,128)} %param.20) | copy-start | bytes 786436
  45.0 105.5 %copy-start.18 = (f32[4,4,4]{2,1,0:T(4,128)S(1)}, f32[4,4,4]{2,1,0:T(4,128)}, u32[]{:S(2)}) copy-start(f32[4,4,4]{2,1,0:T(4,128)} %param.19) | copy-start | bytes 772
  45.0 105.6 %copy-start.17 = (f32[2,4,16,192]{3,2,1,0:T(8,128)S(1)}, f32[2,4,16,192]{3,2,1,0:T(8,128)}, u32[]{:S(2)}) copy-start(f32[2,4,16,192]{3,2,1,0:T(8,128)} %param.21) | copy-start | bytes 294916
  45.0 192.3 %all-to-all-start.1 = ((bf16[16,128,2048]{2,1,0:T(8,128)(2,1)}), bf16[16,128,2048]{2,1,0:T(8,128)(2,1)}, u32[]{:S(2)}, u32[]{:S(2)}) async-start(bf16[16,128,2048]{2,1,0:T(8,128)(2,1)} %fusion), calls=%async_computation.1 | async-start | bytes 16777216 | tf_op jit(solution)/shard_map/all_to_all | solution.py:142
  151.4 41.1 %copy-start.7 = (bf16[64,768]{1,0:T(8,128)(2,1)}, bf16[64,768]{1,0:T(8,128)(2,1)S(1)}, u32[]{:S(2)}) copy-start(bf16[64,768]{1,0:T(8,128)(2,1)S(1)} %convert_element_type.143) | copy-start | bytes 294916
  153.3 43.2 %copy-start.8 = (bf16[64,768]{1,0:T(8,128)(2,1)}, bf16[64,768]{1,0:T(8,128)(2,1)S(1)}, u32[]{:S(2)}) copy-start(bf16[64,768]{1,0:T(8,128)(2,1)S(1)} %convert_element_type.134) | copy-start | bytes 294916
  185.6 7.5 %slice-start = ((s8[6291456]{0:T(1024)(128)(4,1)}), s8[4194304]{0:T(1024)(128)(4,1)S(1)}, s32[]{:S(2)}) async-start(s8[6291456]{0:T(1024)(128)(4,1)} %bitcast.251), calls=%async_computation.4 | async-start | bytes 8388608
  186.9 9.6 %copy-start.13 = (bf16[1024,64]{0,1:T(8,128)(2,1)}, bf16[1024,64]{0,1:T(8,128)(2,1)S(1)}, u32[]{:S(2)}) copy-start(bf16[1024,64]{0,1:T(8,128)(2,1)S(1)} %fusion.48) | copy-start | bytes 393220
  193.1 16.6 %copy-start.2 = (f32[1024,768]{1,0:T(8,128)}, f32[1024,768]{1,0:T(8,128)S(1)}, u32[]{:S(2)}) copy-start(f32[1024,768]{1,0:T(8,128)S(1)} %convolution_add_fusion) | copy-start | bytes 9437188
  197.2 8.7 %copy-start.1 = (f32[1024,768]{1,0:T(8,128)}, f32[1024,768]{1,0:T(8,128)S(1)}, u32[]{:S(2)}) copy-start(f32[1024,768]{1,0:T(8,128)S(1)} %convolution_add_fusion.1) | copy-start | bytes 9437188
  197.2 8.7 %slice-start.4 = ((s8[6291456]{0:T(1024)(128)(4,1)}), s8[4194304]{0:T(1024)(128)(4,1)S(1)}, s32[]{:S(2)}) async-start(s8[6291456]{0:T(1024)(128)(4,1)} %bitcast.255), calls=%async_computation.8 | async-start | bytes 8388608
  237.3 120.5 %all-to-all-start = ((bf16[2,1024,2048]{2,0,1:T(2,128)(2,1)}), bf16[2,1024,2048]{2,0,1:T(2,128)(2,1)}, u32[]{:S(2)}, u32[]{:S(2)}) async-start(bf16[2,1024,2048]{2,0,1:T(2,128)(2,1)} %copy.114), calls=%async_computation | async-start | bytes 16777216 | tf_op jit(solution)/shard_map/all_to_all | solution.py:128
  242.4 112.2 %all-reduce.7.cloned.1.call-start = ((), (), s32[]{:S(2)}) async-start(), calls=%async_computation.3 | async-start | bytes 786432 | tf_op jit(solution)/shard_map/psum | solution.py:172
  243.3 6.8 %copy-start.25 = (f32[1024,768]{1,0:T(8,128)S(1)}, f32[1024,768]{1,0:T(8,128)}, u32[]{:S(2)}) copy-start(f32[1024,768]{1,0:T(8,128)} %fusion.9) | copy-start | bytes 9437188
  256.8 9.0 %copy-start.14 = (bf16[1024,64]{0,1:T(8,128)(2,1)S(1)}, bf16[1024,64]{0,1:T(8,128)(2,1)}, u32[]{:S(2)}) copy-start(bf16[1024,64]{0,1:T(8,128)(2,1)} %copy-done.13) | copy-start | bytes 393220
  273.1 7.3 %copy-start.4 = (f32[4,16,4,192]{3,2,1,0:T(4,128)S(1)}, f32[4,16,4,192]{3,2,1,0:T(4,128)}, u32[]{:S(2)}) copy-start(f32[4,16,4,192]{3,2,1,0:T(4,128)} %reshape.274) | copy-start | bytes 589828
  274.5 9.5 %copy-start.12 = (f32[1,4,16,192]{3,2,1,0:T(8,128)S(1)}, f32[1,4,16,192]{3,2,1,0:T(8,128)}, u32[]{:S(2)}) copy-start(f32[1,4,16,192]{3,2,1,0:T(8,128)} %copy-done.11) | copy-start | bytes 147460
  274.5 10.5 %copy-start.10 = (f32[1,4,16,192]{3,2,1,0:T(8,128)S(1)}, f32[1,4,16,192]{3,2,1,0:T(8,128)}, u32[]{:S(2)}) copy-start(f32[1,4,16,192]{3,2,1,0:T(8,128)} %copy-done.9) | copy-start | bytes 147460
  274.6 11.4 %copy-start.6 = (f32[1,4,512,16]{2,3,1,0:T(8,128)S(1)}, f32[1,4,512,16]{2,3,1,0:T(8,128)}, u32[]{:S(2)}) copy-start(f32[1,4,512,16]{2,3,1,0:T(8,128)} %copy-done.5) | copy-start | bytes 393220
  357.9 10.6 %copy-start.21 = (s32[1024]{0:T(1024)S(1)}, s32[1024]{0:T(1024)}, u32[]{:S(2)}) copy-start(s32[1024]{0:T(1024)} %broadcast_clamp_fusion.3) | copy-start | bytes 12292
  368.5 13.3 %copy-start.15 = (f32[128,8]{1,0:T(8,128)S(1)}, f32[128,8]{1,0:T(8,128)}, u32[]{:S(2)}) copy-start(f32[128,8]{1,0:T(8,128)} %copy.119) | copy-start | bytes 12292
  (12 other events, 47.1 us)
Sparse Core Ops, SparseCore 0:
  9.9 39.4 all-gather.1
  284.1 39.6 all-reduce.6
where the time goes:
time: 401 us; the launch traced here: 396 us
  blocking collectives  161 us (40%)
  local copies, waits for them, and re-layouts  112 us (28%)
  matrix products  69.4 us (17%)
  other arithmetic  27.7 us (7%)
  between operations  15.1 us (4%)
  starting transfers between devices  10.5 us (3%)
    all_gather x1, blocking collectives, on_device(): lax.all_gather(expert_ids, 'expert', axis=0, tiled=True)  96.9 us
    psum x1, blocking collectives, on_device(): adown_total, aup_total = lax.psum((adown_total, aup_total), 'expert')  43.9 us
    psum x1, blocking collectives, on_device(): lax.psum((bdown_all, bup_all, adown_total, aup_total), 'dp')  19.9 us
    gather x1, local copies, waits for them, and re-layouts, on_device(): padded[(global_slot // top_k).reshape(-1)]  19.5 us
    another operation x1, local copies, waits for them, and re-layouts, on_device(): jnp.stack(outputs)  16.4 us
    dot_general x2, matrix products, expert_backward(): lax.dot_general(weighted, down_mat, (((1,), (1,)), ((), ())), preferred_e...  15.1 us
    gather x1, local copies, waits for them, and re-layouts, on_device(): returned.reshape(expert_count * capacity, model_width)[own_position]  13.3 us
    gather x1, local copies, waits for them, and re-layouts, on_device(): gate_pad[own_map].astype(jnp.float32)[:, None]  13.1 us
  transfers between devices with their start and end apart: 4, of which 0 were waited for; matrix products, arithmetic and copies ran while one was open for 44% of the time, Pallas kernels for 0%

commit v1 on v0

--- a/solution.py
+++ b/solution.py
@@ -3,6 +3,8 @@
 import jax
 import jax.numpy as jnp
 from jax import lax
+from jax.experimental import pallas as pl
+from jax.experimental.pallas import tpu as pltpu
 from jax.sharding import PartitionSpec as P
 
 
@@ -176,9 +178,277 @@
     return (mixed, bdown_all, bup_all, adown_total, aup_total)
 
 
+def group_kernel(
+    tok_ref, grad_ref, ids_ref, probs_ref, adt_ref, aup_ref, gate_hbm, up_hbm, down_hbm,
+    mixed_ref, gat_ref, gb_ref,
+    xs, gs, gate_v, up_v, down_v, coef, low_v, hid, part, twin_in, mixed_in,
+    w_sem, tok_send, tok_recv, gr_send, gr_recv, tw_send, tw_recv, mx_send, mx_recv,
+):
+    f32, bf16 = jnp.float32, jnp.bfloat16
+    rows, width = tok_ref.shape
+    ff = gate_v.shape[2]
+    chunk = 256
+    me = lax.axis_index("expert")
+    core = me % 2
+    other = 1 - core
+    xpos = (me // 2) % 2
+    ypos = me // 4
+    twin = me + 1 - 2 * core
+    x_dev = me + 2 - 4 * xpos
+    y_dev = me + 4 - 8 * ypos
+    d_dev = x_dev + 4 - 8 * ypos
+    peers = (twin, x_dev, y_dev, d_dev)
+
+    loads = [
+        pltpu.make_async_copy(gate_hbm, gate_v, w_sem.at[0]),
+        pltpu.make_async_copy(up_hbm, up_v, w_sem.at[1]),
+        pltpu.make_async_copy(down_hbm, down_v, w_sem.at[2]),
+    ]
+    for load in loads:
+        load.start()
+    barrier = pltpu.get_barrier_semaphore()
+    for peer in peers:
+        pl.semaphore_signal(
+            barrier, inc=1, device_id={"expert": peer}, device_id_type=pl.DeviceIdType.MESH
+        )
+
+    lanes = lax.broadcasted_iota(jnp.int32, (rows, 128), 1)
+    weights = jnp.zeros((rows, 128), f32)
+    for k in range(ids_ref.shape[1]):
+        weights = weights + jnp.where(
+            ids_ref[:, k : k + 1] == lanes, probs_ref[:, k : k + 1].astype(f32), 0.0
+        )
+    xs[0, core, :, :width] = tok_ref[...]
+    xs[0, core, :, width:] = weights.astype(bf16)
+    gs[0, core] = grad_ref[...]
+    pl.semaphore_wait(barrier, len(peers))
+
+    def remote(src, dst, send, recv, device):
+        return pltpu.make_async_remote_copy(
+            src_ref=src, dst_ref=dst, send_sem=send, recv_sem=recv,
+            device_id={"expert": device}, device_id_type=pl.DeviceIdType.MESH,
+        )
+
+    def gather_copies(buf, send, recv, via_x):
+        pick = lambda slot, to, n: remote(
+            buf.at[slot[0], core], buf.at[slot[1], core], send.at[n], recv.at[n], to
+        )
+        copies = [pick((r, r), twin, r) for r in range(4)]
+        copies.append(pick((0, 1), x_dev, 4))
+        copies.append(pick((0, 2), y_dev, 5))
+        copies.append(pick((1, 3), y_dev, 6) if via_x else pick((2, 3), x_dev, 6))
+        return copies
+
+    tok = gather_copies(xs, tok_send, tok_recv, True)
+    grd = gather_copies(gs, gr_send, gr_recv, False)
+    pair = [
+        remote(part.at[r, other], twin_in.at[r], tw_send.at[r], tw_recv.at[r], twin)
+        for r in range(4)
+    ]
+    back = [
+        remote(part.at[r, core], mixed_in.at[r], mx_send.at[r], mx_recv.at[r], dev)
+        for r, dev in ((1, x_dev), (2, y_dev), (3, d_dev))
+    ]
+
+    nt = (((1,), (1,)), ((), ()))
+
+    def forward(r):
+        x = lambda: xs[r, :, :, :width].reshape(2 * rows, width)
+        low_v[r] = lax.dot_general(x(), adt_ref[...], nt, preferred_element_type=f32).astype(bf16)
+        table = xs[r, :, :, width:].reshape(2 * rows, 128).astype(f32)
+        at = lax.broadcasted_iota(jnp.int32, (2 * rows, 128), 1)
+        for e in range(2):
+            weight = jnp.sum(jnp.where(at == 2 * me + e, table, 0.0), axis=1, keepdims=True)
+
+            def step(c, carry):
+                here = pl.ds(pl.multiple_of(c * chunk, chunk), chunk)
+                wide = pl.ds(pl.multiple_of(e * ff + c * chunk, chunk), chunk)
+                gate = jnp.dot(x(), gate_v[e, :, here], preferred_element_type=f32)
+                gate = gate + jnp.dot(low_v[r], aup_ref[:, wide], preferred_element_type=f32)
+                up = jnp.dot(x(), up_v[e, :, here], preferred_element_type=f32)
+                sig = 1.0 / (1.0 + jnp.exp(-gate))
+                scaled = weight * up * sig
+                hid[:, wide] = (scaled * gate).astype(bf16)
+                coef[r, :, wide] = scaled * (1.0 + gate * (1.0 - sig))
+                return carry
+
+            lax.fori_loop(0, ff // chunk, step, 0)
+
+        def out_step(c, carry):
+            here = pl.ds(pl.multiple_of(c * chunk, chunk), chunk)
+            out = jnp.dot(hid[...], down_v[:, here], preferred_element_type=f32)
+            part[r, :, :, here] = out.astype(bf16).reshape(2, rows, chunk)
+            return carry
+
+        lax.fori_loop(0, width // chunk, out_step, 0)
+
+    def backward(r):
+        def step(c, carry):
+            here = pl.ds(pl.multiple_of(c * chunk, chunk), chunk)
+            grad = lax.dot_general(
+                gs[r].reshape(2 * rows, width), down_v[here, :], nt, preferred_element_type=f32
+            )
+            hid[:, here] = (grad * coef[r, :, here]).astype(bf16)
+            return carry
+
+        lax.fori_loop(0, 2 * ff // chunk, step, 0)
+        low_grad = lax.dot_general(hid[...], aup_ref[...], nt, preferred_element_type=f32)
+        low_grad_t = low_grad.T.astype(bf16)
+        low_t = low_v[r].astype(f32).T.astype(bf16)
+        up_part = jnp.dot(low_t, hid[...], preferred_element_type=f32)
+        down_part = jnp.dot(
+            low_grad_t, xs[r, :, :, :width].reshape(2 * rows, width), preferred_element_type=f32
+        )
+        if r == 0:
+            gb_ref[...] = up_part
+            gat_ref[...] = down_part
+        else:
+            gb_ref[...] += up_part
+            gat_ref[...] += down_part
+
+    def combine(r):
+        pair[r].wait()
+        part[r, core] = (part[r, core].astype(f32) + twin_in[r].astype(f32)).astype(bf16)
+        if r:
+            back[r - 1].start()
+
+    for n in (4, 5, 0):
+        tok[n].start()
+    for load in loads[:2]:
+        load.wait()
+    tok[0].wait_recv()
+    loads[2].wait()
+    forward(0)
+    pair[0].start()
+    tok[4].wait_recv()
+    tok[6].start()
+    tok[1].start()
+    tok[5].wait_recv()
+    tok[2].start()
+    for n in (5, 4, 0):
+        grd[n].start()
+    tok[1].wait_recv()
+    forward(1)
+    pair[1].start()
+    tok[6].wait_recv()
+    tok[3].start()
+    tok[2].wait_recv()
+    forward(2)
+    pair[2].start()
+    combine(1)
+    grd[5].wait_recv()
+    grd[6].start()
+    grd[2].start()
+    tok[3].wait_recv()
+    forward(3)
+    pair[3].start()
+    combine(2)
+    grd[4].wait_recv()
+    grd[1].start()
+    grd[0].wait_recv()
+    backward(0)
+    combine(3)
+    combine(0)
+    grd[6].wait_recv()
+    grd[3].start()
+    grd[1].wait_recv()
+    backward(1)
+    grd[2].wait_recv()
+    backward(2)
+    grd[3].wait_recv()
+    backward(3)
+    total = part[0, core].astype(f32)
+    for n in range(3):
+        back[n].wait()
+        total = total + mixed_in[n + 1].astype(f32)
+    mixed_ref[...] = total.astype(bf16)
+    for copy in tok + grd:
+        copy.wait_send()
+
+
+def fused_device(
+    tokens, grad_mixed, expert_ids, gate_probs, gate_proj, up_proj, down_proj,
+    share_down, share_up, factor_down, factor_up,
+):
+    f32, bf16 = jnp.float32, jnp.bfloat16
+    rows, width = tokens.shape
+    members, ff = gate_proj.shape[0], gate_proj.shape[2]
+    high = lax.Precision.HIGHEST
+    adt = jnp.einsum("iac,eibd->ecdab", share_down, factor_down, precision=high)
+    adt = adt.reshape(-1, width).astype(bf16)
+    rank = adt.shape[0] // members
+    ups = jnp.einsum("iac,eibd->eabcd", share_up, factor_up, precision=high)
+    ups = ups.reshape(members, rank, ff).astype(bf16)
+    aup = jnp.zeros((members * rank, members * ff), bf16)
+    for e in range(members):
+        aup = aup.at[e * rank : (e + 1) * rank, e * ff : (e + 1) * ff].set(ups[e])
+    vmem = pl.BlockSpec(memory_space=pltpu.VMEM)
+    hbm = pl.BlockSpec(memory_space=pl.ANY)
+    dma = pltpu.SemaphoreType.DMA
+    pairs = members * 4 * 2 * rows
+    mixed, gat, gb = pl.pallas_call(
+        group_kernel,
+        out_shape=(
+            jax.ShapeDtypeStruct((rows, width), bf16),
+            jax.ShapeDtypeStruct((members * rank, width), f32),
+            jax.ShapeDtypeStruct((members * rank, members * ff), f32),
+        ),
+        in_specs=[vmem] * 6 + [hbm] * 3,
+        out_specs=(vmem, vmem, vmem),
+        scratch_shapes=[
+            pltpu.VMEM((4, 2, rows, width + 128), bf16),
+            pltpu.VMEM((4, 2, rows, width), bf16),
+            pltpu.VMEM((members, width, ff), bf16),
+            pltpu.VMEM((members, width, ff), bf16),
+            pltpu.VMEM((members * ff, width), bf16),
+            pltpu.VMEM((4, 2 * rows, members * ff), f32),
+            pltpu.VMEM((4, 2 * rows, members * rank), bf16),
+            pltpu.VMEM((2 * rows, members * ff), bf16),
+            pltpu.VMEM((4, 2, rows, width), bf16),
+            pltpu.VMEM((4, rows, width), bf16),
+            pltpu.VMEM((4, rows, width), bf16),
+            dma((3,)), dma((7,)), dma((7,)), dma((7,)), dma((7,)),
+            dma((4,)), dma((4,)), dma((4,)), dma((4,)),
+        ],
+        compiler_params=pltpu.CompilerParams(
+            collective_id=0, has_side_effects=True, vmem_limit_bytes=58 * 1024 * 1024
+        ),
+        cost_estimate=pl.CostEstimate(
+            flops=8 * pairs * width * ff, bytes_accessed=6 * members * width * ff,
+            transcendentals=pairs * ff,
+        ),
+    )(
+        tokens, grad_mixed, expert_ids, gate_probs, adt, aup,
+        gate_proj, up_proj, down_proj.reshape(members * ff, width),
+    )
+    return finish(mixed, gat, gb, share_down, share_up, factor_down, factor_up)
+
+
+def finish(mixed, gat, gb, share_down, share_up, factor_down, factor_up):
+    high = lax.Precision.HIGHEST
+    members, kron_n, rows_d, cols_d = factor_down.shape
+    rows_u, cols_u = factor_up.shape[2:]
+    rank, ff = kron_n * rows_u, kron_n * cols_u
+    blocks_d = gat.reshape(members, kron_n, cols_d, kron_n, rows_d)
+    blocks_u = jnp.stack(
+        [gb[e * rank : (e + 1) * rank, e * ff : (e + 1) * ff] for e in range(members)]
+    ).reshape(members, kron_n, rows_u, kron_n, cols_u)
+    bd = jnp.einsum("iac,ecdab->eibd", share_down, blocks_d, precision=high)
+    sd = jnp.einsum("eibd,ecdab->iac", factor_down, blocks_d, precision=high)
+    bu = jnp.einsum("iac,eabcd->eibd", share_up, blocks_u, precision=high)
+    su = jnp.einsum("eibd,eabcd->iac", factor_up, blocks_u, precision=high)
+    flat = jnp.concatenate([v.reshape(-1) for v in (bd, bu)])
+    flat = lax.psum(flat, "dp")
+    small = lax.psum(jnp.stack([sd, su]), ("dp", "expert"))
+    bd_all = flat[: bd.size].reshape(bd.shape)
+    bu_all = flat[bd.size :].reshape(bu.shape)
+    return (mixed, bd_all, bu_all, small[0], small[1])
+
+
 def solution(mesh):
+    body = fused_device if mesh.shape["expert"] == 8 else on_device
     return jax.shard_map(
-        on_device,
+        body,
         mesh=mesh,
         in_specs=(
             P(("dp", "expert"), None),

time: 401 us -> 171 us (0.43); the launches traced: 396 us -> 170 us
  blocking collectives: 161 us -> 39.8 us
  local copies, waits for them, and re-layouts: 112 us -> 19.9 us
  Pallas kernels: 0 us -> 81 us
  matrix products: 69.4 us -> 13.7 us
  other arithmetic: 27.7 us -> 1.83 us
  starting transfers between devices: 10.5 us -> 0.04 us
    all_gather x1 -> x0, blocking collectives: 96.9 us -> none  [on_device(): lax.all_gather(expert_ids, 'expert', axis=0, tiled=True)]
    pallas_call x0 -> x1, Pallas kernels: none -> 81 us  [fused_device(): pl.pallas_call(group_kernel, out_shape=(jax.ShapeDtypeStruct((rows, width...]
    gather x4 -> x0, local copies, waits for them, and re-layouts: 56.9 us -> none  [the longest x1 19.5 us: on_device(): padded[(global_slot // top_k).reshape(-1)]]
    dot_general x30 -> x6, matrix products: 69.4 us -> 13.7 us  [the longest x1 3.41 us: finish(): sd = jnp.einsum('eibd,ecdab->iac', factor_down, blocks_d, precision=high)]
    psum x2 -> x1, blocking collectives: 63.8 us -> 39.8 us  [finish(): small = lax.psum(jnp.stack([sd, su]), ('dp', 'expert'))]
    another operation x1 -> x5, local copies, waits for them, and re-layouts: 16.4 us -> 0.69 us  [the longest x3 0.43 us: finish(): jnp.stack([gb[e * rank:(e + 1) * rank, e * ff:(e + 1) * ff] for e in rang...]
    all_to_all x1 -> x0, local copies, waits for them, and re-layouts: 10.6 us -> none  [on_device(): lax.all_to_all(jnp.stack(outputs), 'expert', split_axis=1, concat_axis=0,...]
    all_to_all x2 -> x0, starting transfers between devices: 10.4 us -> none  [the longest x1 5.38 us: on_device(): lax.all_to_all(weighted.reshape(expert_count, capacity, model_width), 'ex...]
  transfers between devices with their start and end apart: 4 -> 1, of which waited for: 0 -> 0; matrix products, arithmetic and copies ran while one was open for 44% -> 4% of each run, Pallas kernels for 0% -> 0%
where the time goes in v1:
time: 171 us; the launch traced here: 170 us
  Pallas kernels  81 us (47%)
  blocking collectives  39.8 us (23%)
  local copies, waits for them, and re-layouts  19.9 us (12%)
  between operations  14.2 us (8%)
  matrix products  13.7 us (8%)
  other arithmetic  1.83 us (1%)
    pallas_call x1, Pallas kernels, fused_device(): pl.pallas_call(group_kernel, out_shape=(jax.ShapeDtypeStruct((rows, width...  81 us
    psum x1, blocking collectives, finish(): small = lax.psum(jnp.stack([sd, su]), ('dp', 'expert'))  39.8 us
    unnamed x19, local copies, waits for them, and re-layouts  8.15 us
  transfers between devices with their start and end apart: 1, of which 0 were waited for; matrix products, arithmetic and copies ran while one was open for 4% of the time, Pallas kernels for 0%

profile of v1, /device:TPU:0, one launch (start us, length us, event | category | flops | bytes accessed | tf_op | source)
XLA Modules:
  0.0 170.4 jit_solution(10642963442491948686)
XLA Ops:
  7.2 0.8 copy.64
  8.0 1.4 copy.44.probs_ref
  9.4 1.4 copy.43.ids_ref
  10.8 1.9 %fusion.1 = bf16[2,4,16,4,192]{4,3,1,2,0:T(4,128)(2,1)S(1)} fusion(f32[2,4,16,192,1]{3,2,1,0,4:T(8,128)} %bitcast.65, f32[4,4,4,1,1]{2,1,0,4,3:T(4,128)} %bitcast.71), kind=kOutput, calls=%fused_computation.4 | convolution fusion | flops 4816896 | bytes 295168 | tf_op jit(solution)/shard_map/iac,eibd->eabcd/dot_general | solution.py:380
  13.2 2.8 %fusion = bf16[2,4,16,4,512]{4,1,3,2,0:T(4,128)(2,1)S(1)} fusion(f32[2,4,512,16,1]{2,3,1,0,4:T(8,128)} %bitcast.62, f32[4,4,4,1,1]{2,1,0,4,3:T(4,128)} %bitcast.68), kind=kOutput, calls=%fused_computation.1 | convolution fusion | flops 12845056 | bytes 786688 | tf_op jit(solution)/shard_map/iac,eibd->ecdab/dot_general | solution.py:377
  16.3 0.9 copy.94
  17.2 0.7 copy-done.4
  18.0 81.0 %shard_map.146 = (bf16[128,2048]{1,0:T(8,128)(2,1)}, f32[128,2048]{1,0:T(8,128)}, f32[128,1536]{1,0:T(8,128)}) custom-call(bf16[128,2048]{1,0:T(8,128)(2,1)} %tok_ref.1, bf16[128,2048]{1,0:T(8,128)(2,1)} %grad_ref.1, s32[128,8]{1,0:T(8,128)} %copy.43.ids_ref, bf16[128,8]{1,0:T(8,128)(2,1)} %copy.44.probs_ref, bf16[128,2048]{1,0:T(8,128)(2,1)} %bitcast.64, ...), custom_call_target="tpu_custom_call" | custom-call | flops 25769803776 | bytes 18874368 | tf_op jit(solution)/shard_map/pallas_call | solution.py:389
  98.9 1.1 fusion.12
  100.5 0.8 copy-done
  101.9 0.7 reshape.111
  102.7 1.9 %reshape.109 = f32[2,4,16,4,512]{4,3,2,1,0:T(4,128)S(1)} reshape(f32[128,2048]{1,0:T(8,128)} %get-tuple-element.33) | data formatting | bytes 2097152 | tf_op jit(solution)/shard_map/reshape | solution.py:432
  104.6 2.3 %convolution_bitcast_fusion = f32[2,4,512,16]{2,1,3,0:T(4,128)} fusion(f32[2,4,16,4,512]{4,3,2,1,0:T(4,128)S(1)} %reshape.109, f32[4,4,4,1,1]{0,1,2,4,3:T(4,128)S(1)} %copy.64), kind=kOutput, calls=%fused_computation.3 | convolution fusion | flops 12582912 | bytes 1310976 | tf_op jit(solution)/shard_map/iac,ecdab->eibd/dot_general | solution.py:436
  106.9 1.6 copy.47
  108.5 1.3 reshape.110
  109.7 1.8 %pad_maximum_fusion = f32[90112]{0:T(1024)} fusion(f32[24576]{0:T(1024)} %reshape.111, f32[65536]{0:T(1024)} %reshape.110), kind=kLoop, calls=%fused_computation.9 | loop fusion | flops 90112 | bytes 720896 | tf_op jit(solution)/shard_map/concatenate | solution.py:440
  111.6 3.4 %convolution_bitcast_fusion.3 = f32[4,4,4]{0,1,2:T(4,128)S(1)} fusion(f32[2,4,16,4,512]{4,3,2,1,0:T(4,128)S(1)} %reshape.109, f32[2,4,512,16,1]{2,3,1,0,4:T(8,128)S(1)} %bitcast.63), kind=kOutput, calls=%fused_computation.7 | convolution fusion | flops 12582912 | bytes 1310976 | tf_op jit(solution)/shard_map/eibd,ecdab->iac/dot_general | solution.py:437
  115.0 2.6 %convolution_bitcast_fusion.2 = f32[4,4,4]{0,2,1:T(4,128)S(1)} fusion(f32[2,4,16,4,192]{4,3,2,1,0:T(4,128)} %copy-done, f32[2,4,16,192,1]{3,2,1,0,4:T(8,128)S(1)} %bitcast.66), kind=kOutput, calls=%fused_computation.6 | convolution fusion | flops 4718592 | bytes 491776 | tf_op jit(solution)/shard_map/eibd,eabcd->iac/dot_general | solution.py:439
  117.8 39.8 %psum.15 = f32[2,4,4,4]{3,2,1,0:T(4,128)S(1)} all-reduce(f32[2,4,4,4]{3,2,1,0:T(4,128)S(1)} %pad_maximum_fusion.1), channel_id=1, replica_groups=mesh['dp'=4,'expert'=8] {'dp','expert'}, use_global_device_ids=true, to_apply=%region_1.0 | all-reduce | flops 128 | bytes 1024 | tf_op jit(solution)/shard_map/psum | solution.py:442
  158.3 0.9 slice.80
  159.2 0.7 reshape.113
  159.9 1.0 slice.79
  161.5 1.3 copy.58
  162.8 0.8 copy.117
  (32 shorter events, 3.3 us)
Async XLA Ops:
  7.2 151.1 %all-reduce.3.cloned.1.call-start = ((), (), s32[]{:S(2)}) async-start(), calls=%async_computation | async-start | bytes 720896 | tf_op jit(solution)/shard_map/psum | solution.py:441
  17.2 0.7 copy-start.4
  17.9 83.3 %copy-start.5 = (f32[4,4,4]{2,1,0:T(4,128)S(1)}, f32[4,4,4]{2,1,0:T(4,128)}, u32[]{:S(2)}) copy-start(f32[4,4,4]{2,1,0:T(4,128)} %param.23) | copy-start | bytes 772
  100.0 11.6 %copy-start.1 = (f32[2,4,512,16]{2,3,1,0:T(8,128)S(1)}, f32[2,4,512,16]{2,3,1,0:T(8,128)}, u32[]{:S(2)}) copy-start(f32[2,4,512,16]{2,3,1,0:T(8,128)} %param.24) | copy-start | bytes 786436
  100.4 14.6 %copy-start.3 = (f32[2,4,16,192]{3,2,1,0:T(8,128)S(1)}, f32[2,4,16,192]{3,2,1,0:T(8,128)}, u32[]{:S(2)}) copy-start(f32[2,4,16,192]{3,2,1,0:T(8,128)} %param.25) | copy-start | bytes 294916
  100.5 0.8 copy-start
  109.7 53.1 %copy-start.2 = (bf16[128,2048]{1,0:T(8,128)(2,1)S(1)}, bf16[128,2048]{1,0:T(8,128)(2,1)}, u32[]{:S(2)}) copy-start(bf16[128,2048]{1,0:T(8,128)(2,1)} %get-tuple-element.51) | copy-start | bytes 1572868
Sparse Core Ops, SparseCore 0:
  111.7 36.1 all-reduce.2

commit v2 on v1

--- a/solution.py
+++ b/solution.py
@@ -179,10 +179,12 @@
 
 
 def group_kernel(
-    tok_ref, grad_ref, ids_ref, probs_ref, adt_ref, aup_ref, gate_hbm, up_hbm, down_hbm,
-    mixed_ref, gat_ref, gb_ref,
+    sd_ref, su_ref, tok_ref, grad_ref, ids_ref, probs_ref, fd_ref, fu_ref, gate_hbm, up_hbm, down_hbm,
+    mixed_ref, fdown_ref, fup_ref, share_ref,
+    adt_ref, aup_ref, gat_ref, gb_ref, terms, share_parts, share_in, share_hop, scat_out, scat_in, whole,
     xs, gs, gate_v, up_v, down_v, coef, low_v, hid, part, twin_in, mixed_in,
     w_sem, tok_send, tok_recv, gr_send, gr_recv, tw_send, tw_recv, mx_send, mx_recv,
+    sc_send, sc_recv, ga_send, ga_recv, sh_send, sh_recv, hop_send, hop_recv,
 ):
     f32, bf16 = jnp.float32, jnp.bfloat16
     rows, width = tok_ref.shape
@@ -198,6 +200,13 @@
     y_dev = me + 4 - 8 * ypos
     d_dev = x_dev + 4 - 8 * ypos
     peers = (twin, x_dev, y_dev, d_dev)
+    dp = lax.axis_index("dp")
+    n_dp = scat_in.shape[0]
+    others = [lax.rem(dp + j, n_dp) for j in range(1, n_dp)]
+    kron_n, cols_d, rows_d = fd_ref.shape[1:]
+    rows_u, cols_u = fu_ref.shape[2:]
+    rank = kron_n * cols_d
+    mesh_id = pl.DeviceIdType.MESH
 
     loads = [
         pltpu.make_async_copy(gate_hbm, gate_v, w_sem.at[0]),
@@ -209,38 +218,46 @@
     barrier = pltpu.get_barrier_semaphore()
     for peer in peers:
         pl.semaphore_signal(
-            barrier, inc=1, device_id={"expert": peer}, device_id_type=pl.DeviceIdType.MESH
+            barrier, inc=1, device_id={"expert": peer}, device_id_type=mesh_id
         )
-
-    lanes = lax.broadcasted_iota(jnp.int32, (rows, 128), 1)
-    weights = jnp.zeros((rows, 128), f32)
-    for k in range(ids_ref.shape[1]):
-        weights = weights + jnp.where(
-            ids_ref[:, k : k + 1] == lanes, probs_ref[:, k : k + 1].astype(f32), 0.0
-        )
+    for peer in others:
+        pl.semaphore_signal(barrier, inc=1, device_id={"dp": peer}, device_id_type=mesh_id)
+
+    names = lax.broadcasted_iota(jnp.int32, (128, rows), 0)
+    probs = probs_ref[...].astype(f32)
+    weights = jnp.zeros((128, rows), f32)
+    for k in range(ids_ref.shape[0]):
+        weights = weights + jnp.where(ids_ref[k : k + 1, :] == names, probs[k : k + 1, :], 0.0)
+    weights = weights.T
     xs[0, core, :, :width] = tok_ref[...]
     xs[0, core, :, width:] = weights.astype(bf16)
     gs[0, core] = grad_ref[...]
-    pl.semaphore_wait(barrier, len(peers))
-
-    def remote(src, dst, send, recv, device):
+    pl.semaphore_wait(barrier, len(peers) + len(others))
+
+    def remote(src, dst, send, recv, device, axis="expert"):
         return pltpu.make_async_remote_copy(
             src_ref=src, dst_ref=dst, send_sem=send, recv_sem=recv,
-            device_id={"expert": device}, device_id_type=pl.DeviceIdType.MESH,
+            device_id={axis: device}, device_id_type=mesh_id,
         )
 
-    def gather_copies(buf, send, recv, via_x):
+    def gather_copies(buf, send, recv):
         pick = lambda slot, to, n: remote(
             buf.at[slot[0], core], buf.at[slot[1], core], send.at[n], recv.at[n], to
         )
         copies = [pick((r, r), twin, r) for r in range(4)]
         copies.append(pick((0, 1), x_dev, 4))
         copies.append(pick((0, 2), y_dev, 5))
-        copies.append(pick((1, 3), y_dev, 6) if via_x else pick((2, 3), x_dev, 6))
+        for n, near, dev in ((6, 1, y_dev), (7, 2, x_dev)):
+            span = pl.ds((n - 6) * (rows // 2), rows // 2)
+            copies.append(
+                remote(
+                    buf.at[near, core, span], buf.at[3, core, span], send.at[n], recv.at[n], dev
+                )
+            )
         return copies
 
-    tok = gather_copies(xs, tok_send, tok_recv, True)
-    grd = gather_copies(gs, gr_send, gr_recv, False)
+    tok = gather_copies(xs, tok_send, tok_recv)
+    grd = gather_copies(gs, gr_send, gr_recv)
     pair = [
         remote(part.at[r, other], twin_in.at[r], tw_send.at[r], tw_recv.at[r], twin)
         for r in range(4)
@@ -312,8 +329,89 @@
         if r:
             back[r - 1].start()
 
+    scatter = [
+        remote(scat_out.at[peer], scat_in.at[j], sc_send.at[j], sc_recv.at[j], peer, "dp")
+        for j, peer in enumerate(others, 1)
+    ]
+    collect = [
+        remote(whole.at[dp], whole.at[dp], ga_send.at[j], ga_recv.at[j], peer, "dp")
+        for j, peer in enumerate(others, 1)
+    ]
+    share_out = [
+        remote(share_in.at[dp], share_in.at[dp], sh_send.at[j], sh_recv.at[j], peer, "dp")
+        for j, peer in enumerate(others, 1)
+    ]
+    hops = [
+        remote(share_hop.at[2 * n], share_hop.at[2 * n + 1], hop_send.at[n], hop_recv.at[n], dev)
+        for n, dev in enumerate((twin, x_dev, y_dev))
+    ]
+    mix = lambda ref, i, a, c: ref[(i * kron_n + a) * kron_n + c]
+
+    def expand_adapters():
+        aup_ref[...] = jnp.zeros_like(aup_ref)
+        for e in range(2):
+            for a in range(kron_n):
+                for c in range(kron_n):
+                    block = sum(mix(sd_ref, i, a, c) * fd_ref[e, i] for i in range(kron_n))
+                    adt_ref[
+                        e * rank + c * cols_d : e * rank + (c + 1) * cols_d,
+                        a * rows_d : (a + 1) * rows_d,
+                    ] = block.astype(bf16)
+                strip = [
+                    sum(mix(su_ref, i, a, c) * fu_ref[e, i] for i in range(kron_n))
+                    for c in range(kron_n)
+                ]
+                aup_ref[
+                    e * rank + a * rows_u : e * rank + (a + 1) * rows_u, e * ff : (e + 1) * ff
+                ] = jnp.concatenate(strip, axis=1).astype(bf16)
+
+    def fold(product):
+        half = product[:8]
+        for at in range(8, product.shape[0], 8):
+            half = half + product[at : at + 8]
+        full = half.shape[1] // 128 * 128
+        out = half[:, :128]
+        for at in range(128, full, 128):
+            out = out + half[:, at : at + 128]
+        if full < half.shape[1]:
+            rest = half.shape[1] - full
+            pad = jnp.zeros((8, 128 - rest), f32)
+            out = out + jnp.concatenate([half[:, full:], pad], axis=1)
+        return out
+
+    def contract():
+        down_at = lambda e, a, c: gat_ref[
+            e * rank + c * cols_d : e * rank + (c + 1) * cols_d, a * rows_d : (a + 1) * rows_d
+        ]
+        up_at = lambda e, a, c: gb_ref[
+            e * rank + a * rows_u : e * rank + (a + 1) * rows_u,
+            e * ff + c * cols_u : e * ff + (c + 1) * cols_u,
+        ]
+        sides = ((sd_ref, fd_ref, down_at, 0, rows_d), (su_ref, fu_ref, up_at, rows_d, cols_u))
+        for side, (mixer, factor, block_at, start, wide) in enumerate(sides):
+            tall = factor.shape[2]
+            for e in range(2):
+                totals = [None] * kron_n
+                for a in range(kron_n):
+                    for c in range(kron_n):
+                        block = block_at(e, a, c)
+                        for i in range(kron_n):
+                            term = mix(mixer, i, a, c) * block
+                            totals[i] = term if totals[i] is None else totals[i] + term
+                            place = ((side * kron_n + i) * kron_n + a) * kron_n + c
+                            piece = fold(factor[e, i] * block)
+                            if e:
+                                piece = piece + share_parts[place]
+                            share_parts[place] = piece
+                for i in range(kron_n):
+                    top = (e * kron_n + i) * tall
+                    terms[top : top + tall, start : start + wide] = totals[i]
+        flat = jnp.sum(share_parts[...], axis=1)
+        share_in[dp] = jnp.broadcast_to(jnp.sum(flat.T, axis=0, keepdims=True), (8, 128))
+
     for n in (4, 5, 0):
         tok[n].start()
+    expand_adapters()
     for load in loads[:2]:
         load.wait()
     tok[0].wait_recv()
@@ -324,6 +422,7 @@
     tok[6].start()
     tok[1].start()
     tok[5].wait_recv()
+    tok[7].start()
     tok[2].start()
     for n in (5, 4, 0):
         grd[n].start()
@@ -331,25 +430,28 @@
     forward(1)
     pair[1].start()
     tok[6].wait_recv()
+    tok[7].wait_recv()
     tok[3].start()
     tok[2].wait_recv()
     forward(2)
     pair[2].start()
+    grd[5].wait_recv()
+    grd[7].start()
+    grd[2].start()
+    grd[4].wait_recv()
+    grd[6].start()
+    grd[1].start()
     combine(1)
-    grd[5].wait_recv()
-    grd[6].start()
-    grd[2].start()
     tok[3].wait_recv()
     forward(3)
     pair[3].start()
     combine(2)
-    grd[4].wait_recv()
-    grd[1].start()
     grd[0].wait_recv()
     backward(0)
     combine(3)
     combine(0)
     grd[6].wait_recv()
+    grd[7].wait_recv()
     grd[3].start()
     grd[1].wait_recv()
     backward(1)
@@ -357,11 +459,41 @@
     backward(2)
     grd[3].wait_recv()
     backward(3)
+
+    terms[:, rows_d:] = jnp.zeros_like(terms[:, rows_d:])
+    contract()
+    scat_out[...] = terms[...].astype(bf16).reshape(scat_out.shape)
+    for copy in scatter + share_out:
+        copy.start()
     total = part[0, core].astype(f32)
     for n in range(3):
         back[n].wait()
         total = total + mixed_in[n + 1].astype(f32)
     mixed_ref[...] = total.astype(bf16)
+    span = terms.shape[0] // n_dp
+    own = terms[pl.ds(pl.multiple_of(dp * span, span), span), :]
+    for j, copy in enumerate(scatter, 1):
+        copy.wait()
+        own = own + scat_in[j].astype(f32)
+    whole[dp] = own.astype(bf16)
+    for copy in collect:
+        copy.start()
+    for copy in share_out:
+        copy.wait()
+    share = share_in[0]
+    for j in range(1, n_dp):
+        share = share + share_in[j]
+    for n, copy in enumerate(hops):
+        share_hop[2 * n] = share
+        copy.start()
+        copy.wait()
+        share = share + share_hop[2 * n + 1]
+    share_ref[...] = share
+    for copy in collect:
+        copy.wait()
+    result = whole[...].reshape(terms.shape).astype(f32)
+    fdown_ref[...] = result[:, :rows_d]
+    fup_ref[...] = result[:, rows_d : rows_d + cols_u]
     for copy in tok + grd:
         copy.wait_send()
 
@@ -373,29 +505,39 @@
     f32, bf16 = jnp.float32, jnp.bfloat16
     rows, width = tokens.shape
     members, ff = gate_proj.shape[0], gate_proj.shape[2]
-    high = lax.Precision.HIGHEST
-    adt = jnp.einsum("iac,eibd->ecdab", share_down, factor_down, precision=high)
-    adt = adt.reshape(-1, width).astype(bf16)
-    rank = adt.shape[0] // members
-    ups = jnp.einsum("iac,eibd->eabcd", share_up, factor_up, precision=high)
-    ups = ups.reshape(members, rank, ff).astype(bf16)
-    aup = jnp.zeros((members * rank, members * ff), bf16)
-    for e in range(members):
-        aup = aup.at[e * rank : (e + 1) * rank, e * ff : (e + 1) * ff].set(ups[e])
+    kron_n, rows_d, cols_d = factor_down.shape[1:]
+    rows_u, cols_u = factor_up.shape[2:]
+    rank = kron_n * cols_d
+    n_dp = lax.axis_size("dp")
+    terms = members * kron_n * cols_d
+    padded = rows_d + (cols_u + 127) // 128 * 128
     vmem = pl.BlockSpec(memory_space=pltpu.VMEM)
+    smem = pl.BlockSpec(memory_space=pltpu.SMEM)
     hbm = pl.BlockSpec(memory_space=pl.ANY)
     dma = pltpu.SemaphoreType.DMA
     pairs = members * 4 * 2 * rows
-    mixed, gat, gb = pl.pallas_call(
+    mixed, fdown, fup, share = pl.pallas_call(
         group_kernel,
         out_shape=(
             jax.ShapeDtypeStruct((rows, width), bf16),
-            jax.ShapeDtypeStruct((members * rank, width), f32),
-            jax.ShapeDtypeStruct((members * rank, members * ff), f32),
+            jax.ShapeDtypeStruct((terms, rows_d), f32),
+            jax.ShapeDtypeStruct((terms, cols_u), f32),
+            jax.ShapeDtypeStruct((8, 128), f32),
         ),
-        in_specs=[vmem] * 6 + [hbm] * 3,
-        out_specs=(vmem, vmem, vmem),
+        in_specs=[smem] * 2 + [vmem] * 6 + [hbm] * 3,
+        out_specs=(vmem, vmem, vmem, vmem),
         scratch_shapes=[
+            pltpu.VMEM((members * rank, width), bf16),
+            pltpu.VMEM((members * rank, members * ff), bf16),
+            pltpu.VMEM((members * rank, width), f32),
+            pltpu.VMEM((members * rank, members * ff), f32),
+            pltpu.VMEM((terms, padded), f32),
+            pltpu.VMEM((2 * kron_n**3, 8, 128), f32),
+            pltpu.VMEM((n_dp, 8, 128), f32),
+            pltpu.VMEM((6, 8, 128), f32),
+            pltpu.VMEM((n_dp, terms // n_dp, padded), bf16),
+            pltpu.VMEM((n_dp, terms // n_dp, padded), bf16),
+            pltpu.VMEM((n_dp, terms // n_dp, padded), bf16),
             pltpu.VMEM((4, 2, rows, width + 128), bf16),
             pltpu.VMEM((4, 2, rows, width), bf16),
             pltpu.VMEM((members, width, ff), bf16),
@@ -407,8 +549,10 @@
             pltpu.VMEM((4, 2, rows, width), bf16),
             pltpu.VMEM((4, rows, width), bf16),
             pltpu.VMEM((4, rows, width), bf16),
-            dma((3,)), dma((7,)), dma((7,)), dma((7,)), dma((7,)),
+            dma((3,)), dma((8,)), dma((8,)), dma((8,)), dma((8,)),
             dma((4,)), dma((4,)), dma((4,)), dma((4,)),
+            dma((n_dp,)), dma((n_dp,)), dma((n_dp,)), dma((n_dp,)),
+            dma((n_dp,)), dma((n_dp,)), dma((3,)), dma((3,)),
         ],
         compiler_params=pltpu.CompilerParams(
             collective_id=0, has_side_effects=True, vmem_limit_bytes=58 * 1024 * 1024
@@ -418,31 +562,14 @@
             transcendentals=pairs * ff,
         ),
     )(
-        tokens, grad_mixed, expert_ids, gate_probs, adt, aup,
+        share_down.reshape(-1), share_up.reshape(-1), tokens, grad_mixed,
+        expert_ids.T, gate_probs.T, jnp.swapaxes(factor_down, 2, 3), factor_up,
         gate_proj, up_proj, down_proj.reshape(members * ff, width),
     )
-    return finish(mixed, gat, gb, share_down, share_up, factor_down, factor_up)
-
-
-def finish(mixed, gat, gb, share_down, share_up, factor_down, factor_up):
-    high = lax.Precision.HIGHEST
-    members, kron_n, rows_d, cols_d = factor_down.shape
-    rows_u, cols_u = factor_up.shape[2:]
-    rank, ff = kron_n * rows_u, kron_n * cols_u
-    blocks_d = gat.reshape(members, kron_n, cols_d, kron_n, rows_d)
-    blocks_u = jnp.stack(
-        [gb[e * rank : (e + 1) * rank, e * ff : (e + 1) * ff] for e in range(members)]
-    ).reshape(members, kron_n, rows_u, kron_n, cols_u)
-    bd = jnp.einsum("iac,ecdab->eibd", share_down, blocks_d, precision=high)
-    sd = jnp.einsum("eibd,ecdab->iac", factor_down, blocks_d, precision=high)
-    bu = jnp.einsum("iac,eabcd->eibd", share_up, blocks_u, precision=high)
-    su = jnp.einsum("eibd,eabcd->iac", factor_up, blocks_u, precision=high)
-    flat = jnp.concatenate([v.reshape(-1) for v in (bd, bu)])
-    flat = lax.psum(flat, "dp")
-    small = lax.psum(jnp.stack([sd, su]), ("dp", "expert"))
-    bd_all = flat[: bd.size].reshape(bd.shape)
-    bu_all = flat[bd.size :].reshape(bu.shape)
-    return (mixed, bd_all, bu_all, small[0], small[1])
+    fdown = jnp.swapaxes(fdown.reshape(members, kron_n, cols_d, rows_d), 2, 3)
+    fup = fup.reshape(factor_up.shape)
+    share = share[0].reshape((2,) + share_down.shape)
+    return (mixed, fdown, fup, share[0], share[1])
 
 
 def solution(mesh):

time: 171 us -> 90.8 us (0.53)
  blocking collectives: 39.8 us -> 0 us
  matrix products: 13.7 us -> 0 us
  between operations: 14.2 us -> 0.64 us
  local copies, waits for them, and re-layouts: 19.9 us -> 9.95 us
  other arithmetic: 1.83 us -> 0 us
    psum x1 -> x0, blocking collectives: 39.8 us -> none  [finish(): small = lax.psum(jnp.stack([sd, su]), ('dp', 'expert'))]
    dot_general x6 -> x0, matrix products: 13.7 us -> none  [the longest x1 3.41 us: finish(): sd = jnp.einsum('eibd,ecdab->iac', factor_down, blocks_d, precision=high)]
    unnamed x19 -> x3, local copies, waits for them, and re-layouts: 8.15 us -> 5.12 us
    reshape x5 -> x2, local copies, waits for them, and re-layouts: 5.26 us -> 2.6 us  [the longest x1 1.3 us: fused_device(): share_down.reshape(-1)]
    slice x6 -> x1, local copies, waits for them, and re-layouts: 3.11 us -> 0.83 us  [fused_device(): return (mixed, fdown, fup, share[0], share[1])]
    concatenate x1 -> x0, other arithmetic: 1.82 us -> none  [finish(): flat = jnp.concatenate([v.reshape(-1) for v in (bd, bu)])]
  transfers between devices with their start and end apart: 1 -> 0, of which waited for: 0 -> 0; matrix products, arithmetic and copies ran while one was open for 4% -> 0% of each run, Pallas kernels for 0% -> 0%
where the time goes in v2:
time: 90.8 us; the launch traced here: 90.4 us
  Pallas kernels  79.8 us (88%)
  local copies, waits for them, and re-layouts  9.95 us (11%)
    pallas_call x1, Pallas kernels, fused_device(): pl.pallas_call(group_kernel, out_shape=(jax.ShapeDtypeStruct((rows, width...  79.8 us
    unnamed x3, local copies, waits for them, and re-layouts  5.12 us

profile of v2, /device:TPU:0, one launch (start us, length us, event | category | flops | bytes accessed | tf_op | source)
XLA Modules:
  0.0 90.4 jit_solution(563972454116400859)
XLA Ops:
  0.6 1.3 %reshape.29.sd_ref = f32[64]{0:T(128)} reshape(f32[4,4,4]{2,1,0:T(4,128)} %param.18) | data formatting | bytes 512 | tf_op jit(solution)/shard_map/reshape | solution.py:565
  1.9 1.3 %reshape.30.su_ref = f32[64]{0:T(128)} reshape(f32[4,4,4]{2,1,0:T(4,128)} %param.19) | data formatting | bytes 512 | tf_op jit(solution)/shard_map/reshape | solution.py:565
  3.2 79.8 %shard_map.146 = (bf16[128,2048]{1,0:T(8,128)(2,1)}, f32[128,512]{1,0:T(8,128)}, f32[128,192]{1,0:T(8,128)}, f32[8,128]{1,0:T(8,128)}) custom-call(f32[64]{0:T(128)} %reshape.29.sd_ref, f32[64]{0:T(128)} %reshape.30.su_ref, bf16[128,2048]{1,0:T(8,128)(2,1)} %tok_ref.1, bf16[128,2048]{1,0:T(8,128)(2,1)} %grad_ref.1, s32[8,128]{1,0:T(8,128)} %bitcast.12, ...), custom_call_target="tpu_custom_call" | custom-call | flops 25769803776 | bytes 18874368 | tf_op jit(solution)/shard_map/pallas_call | solution.py:519
  83.1 0.8 slice_reduce_fusion
  83.9 0.7 squeeze.7
  84.6 0.7 squeeze.6
  85.3 1.9 %copy.19 = bf16[128,2048]{1,0:T(8,128)(2,1)} copy(bf16[128,2048]{1,0:T(8,128)(2,1)} %get-tuple-element.20) | data formatting | bytes 1048576
  87.2 1.7 %copy.20 = f32[2,4,512,16]{2,3,1,0:T(8,128)} copy(f32[2,4,512,16]{2,3,1,0:T(8,128)} %bitcast.8) | data formatting | bytes 524288
  88.9 1.6 %copy.21 = f32[2,4,16,192]{3,2,1,0:T(8,128)} copy(f32[2,4,16,192]{3,2,1,0:T(8,128)} %bitcast.9) | data formatting | bytes 196608
